TPU v7x, 256 devices: a whole 4x4x8 slice. The times are simulated.
256 devices in a mesh: scene: 4 (over x), dom: 64 (over z, y, core).
Axes of the slice: x: 4, y: 4, z: 8, core: 2. Of those that a mesh axis runs over, the one named last changes fastest.
Arguments:
- features: bfloat16 [2048, 64, 512], P(('scene', 'dom')), parts along dimension 0, may hold values from -6 to 6
- cotangent: bfloat16 [2048, 64, 512], P(('scene', 'dom')), parts along dimension 0, may hold values from -6 to 6
- weight: bfloat16 [27, 64, 64], replicated, may hold values from -0.15625 to 0.15625
- mask_words: int32 [2048, 18], P(('scene', 'dom')), parts along dimension 0, may hold values from 0 to 1073741823, as said below
- neighbors: int32 [2048, 26], P(('scene', 'dom')), parts along dimension 0, may hold values from -1 to 511, as said below
Outputs:
- out_features: bfloat16 [2048, 64, 512], P(('scene', 'dom')), parts along dimension 0
- in_grad: bfloat16 [2048, 64, 512], P(('scene', 'dom')), parts along dimension 0
- weight_grad: float32 [108, 64, 64], P('scene'), parts along dimension 0
There are 4 independent parts, one for each index of `scene`. A program takes and returns all parts, laid end to end along the dimension named above; an argument that names none is the same for every part. Nothing has to cross between parts.
Inputs may be any that keep to these rules, and one draw needn't show every extreme that they name: `mask_words`: bit r of word w is voxel 30 w + r of the leaf; bits at or past 512 are 0; unused slots have all bits 0. An id is owner * 8 + slot, owner being the index along dom. All leaves at one leaf position along the first dimension have the same owner; a neighbor at first offset -1 is owned by the same device or the one below it, at +1 by the same device or the one above it. The table is symmetric: b is listed as a neighbor of a at offset (p, q, r) exactly when a is listed for b at (-p, -q, -r). Used slots of a device come first; unused slots list no neighbors. At most 4 leaves of one device have a neighbor owned by one given adjacent device, and some device reaches that in every draw; some device uses all 8 slots in every draw.
All inputs are finite; a program needn't handle non-finite values.
Results may differ from a plain program's by a relative error of at most 0.001.
Values may be sent and summed in bfloat16 or wider, within the bound.
A program may use at most 256 MiB of HBM per device.

v0:
```python
import jax
import jax.numpy as jnp
import numpy as np
from jax import lax
from jax.sharding import PartitionSpec as P

LEAF = 8


def with_halo(shard, sides, width):
    for axis, dim in sides:
        size, length = (lax.axis_size(axis), shard.shape[dim])
        up = [(i, (i + 1) % size) for i in range(size - 1)]
        down = [(j, i) for i, j in up]
        last = lax.slice_in_dim(shard, length - width, length, axis=dim)
        leading = lax.slice_in_dim(shard, 0, width, axis=dim)
        before = lax.ppermute(last, axis, up)
        after = lax.ppermute(leading, axis, down)
        shard = jnp.concatenate([before, shard, after], axis=dim)
    return shard


def unpack_voxels(mask_words, voxel_count):
    bit_place = jnp.arange(30, dtype=jnp.int32)
    bit_values = jnp.right_shift(mask_words[:, :, None], bit_place[None, None, :]) & 1
    return bit_values.reshape(mask_words.shape[0], -1)[:, :voxel_count]


def column_of(shift_x, shift_y, shift_z):
    tap_number = (shift_x + 1) * 9 + (shift_y + 1) * 3 + shift_z + 1
    return tap_number if tap_number < 13 else tap_number - 1


def tap_offsets():
    return [
        (shift_x, shift_y, shift_z)
        for shift_x in (-1, 0, 1)
        for shift_y in (-1, 0, 1)
        for shift_z in (-1, 0, 1)
    ]


def axis_cells(shift_value, extent):
    if shift_value < 0:
        return ([0], [extent - 1])
    if shift_value > 0:
        return ([extent + 1], [0])
    return (list(range(1, extent + 1)), list(range(extent)))


def region_tables(offset, extent):
    side = extent + 2
    dest_a, src_a = axis_cells(offset[0], extent)
    dest_b, src_b = axis_cells(offset[1], extent)
    dest_c, src_c = axis_cells(offset[2], extent)
    dest_list = []
    src_list = []
    for index_a in range(len(dest_a)):
        for index_b in range(len(dest_b)):
            for index_c in range(len(dest_c)):
                dest_list.append(
                    (dest_a[index_a] * side + dest_b[index_b]) * side + dest_c[index_c]
                )
                if offset[0] == 0:
                    src_list.append(
                        (src_a[index_a] * extent + src_b[index_b]) * extent + src_c[index_c]
                    )
                else:
                    src_list.append(src_b[index_b] * extent + src_c[index_c])
    return (np.array(dest_list, dtype=np.int32), np.array(src_list, dtype=np.int32))


def take_rows(source, row_index, keep_rows):
    picked = jnp.take(source, jnp.clip(row_index, 0, source.shape[0] - 1), axis=0)
    return jnp.where(keep_rows[:, None, None], picked, jnp.zeros((), source.dtype))


def shards(features, cotangent, weight, mask_words, neighbors):
    leaf_count, channels, voxel_count = features.shape
    edge_cells = LEAF
    side = edge_cells + 2
    padded_cells = side**3
    span_start = side * side + side + 1
    span_cells = padded_cells - 2 * span_start
    face_cells = edge_cells * edge_cells
    device = lax.axis_index("dom")
    occupancy = unpack_voxels(mask_words, voxel_count).astype(features.dtype)
    masked_x = features * occupancy[:, None, :]
    masked_dy = cotangent * occupancy[:, None, :]
    plane_size = channels * face_cells
    low_planes = jnp.stack(
        [
            masked_x[:, :, :face_cells].reshape(leaf_count, plane_size),
            masked_dy[:, :, :face_cells].reshape(leaf_count, plane_size),
        ]
    )
    high_planes = jnp.stack(
        [
            masked_x[:, :, voxel_count - face_cells :].reshape(leaf_count, plane_size),
            masked_dy[:, :, voxel_count - face_cells :].reshape(leaf_count, plane_size),
        ]
    )
    present = neighbors >= 0
    owner_dev = jnp.where(present, neighbors // leaf_count, -2)
    local_here = present & (owner_dev == device)
    from_below = present & (owner_dev == device - 1)
    from_above = present & (owner_dev == device + 1)
    slot_here = neighbors - device * leaf_count
    slot_below = neighbors - (device - 1) * leaf_count
    slot_above = neighbors - (device + 1) * leaf_count
    outgoing = jnp.stack([low_planes, high_planes])
    received = with_halo(outgoing, (("dom", 0),), 1)
    offsets = tap_offsets()
    inner_dest, inner_src = region_tables((0, 0, 0), edge_cells)

    def padded_field(field_number, center):
        pool_high = jnp.concatenate(
            [high_planes[field_number], received[0, field_number]], axis=0
        ).reshape(-1, channels, face_cells)
        pool_low = jnp.concatenate(
            [low_planes[field_number], received[3, field_number]], axis=0
        ).reshape(-1, channels, face_cells)
        padded = (
            jnp.zeros((leaf_count, channels, padded_cells), center.dtype)
            .at[:, :, inner_dest]
            .set(center)
        )
        for offset in offsets:
            if offset == (0, 0, 0):
                continue
            dest_index, src_index = region_tables(offset, edge_cells)
            column = column_of(offset[0], offset[1], offset[2])
            if offset[0] == 0:
                source = jnp.take(center, src_index, axis=2)
                row_index = slot_here[:, column]
                keep_rows = local_here[:, column]
            elif offset[0] < 0:
                source = jnp.take(pool_high, src_index, axis=2)
                row_index = jnp.where(
                    local_here[:, column], slot_here[:, column], leaf_count + slot_below[:, column]
                )
                keep_rows = local_here[:, column] | from_below[:, column]
            else:
                source = jnp.take(pool_low, src_index, axis=2)
                row_index = jnp.where(
                    local_here[:, column], slot_here[:, column], leaf_count + slot_above[:, column]
                )
                keep_rows = local_here[:, column] | from_above[:, column]
            padded = padded.at[:, :, dest_index].set(take_rows(source, row_index, keep_rows))
        return padded

    padded_x = padded_field(0, masked_x)
    padded_dy = padded_field(1, masked_dy)
    span_dy = (
        jnp.zeros((leaf_count, channels, span_cells), masked_dy.dtype)
        .at[:, :, inner_dest - span_start]
        .set(masked_dy)
    )
    shift_list = [(offset[0] * side + offset[1]) * side + offset[2] for offset in offsets]
    group_size = max(1, leaf_count // 8)
    block_count = leaf_count // group_size
    flat_weight = weight.reshape(27 * channels, channels)
    turned_weight = jnp.transpose(weight, (1, 0, 2)).reshape(channels, 27 * channels)

    def block_terms(inputs):
        pad_x_block, pad_dy_block, dy_block = inputs
        stack_x = jnp.concatenate(
            [
                pad_x_block[:, :, span_start + shift : span_start + shift + span_cells]
                for shift in shift_list
            ],
            axis=1,
        )
        stack_dy = jnp.concatenate(
            [
                pad_dy_block[:, :, span_start - shift : span_start - shift + span_cells]
                for shift in shift_list
            ],
            axis=1,
        )
        out_block = jnp.einsum(
            "ko,lkv->lov", flat_weight, stack_x, preferred_element_type=jnp.float32
        )
        back_block = jnp.einsum(
            "ik,lkv->liv", turned_weight, stack_dy, preferred_element_type=jnp.float32
        )
        grad_block = jnp.einsum(
            "lkv,lov->ko", stack_x, dy_block, preferred_element_type=jnp.float32
        )
        return (out_block, back_block, grad_block)

    def regroup(array):
        return array.reshape((block_count, group_size) + array.shape[1:])

    out_parts, back_parts, grad_parts = lax.map(
        block_terms, (regroup(padded_x), regroup(padded_dy), regroup(span_dy))
    )
    out_sum = out_parts.reshape(leaf_count, channels, span_cells)
    back_sum = back_parts.reshape(leaf_count, channels, span_cells)
    grad_local = jnp.sum(grad_parts, axis=0).reshape(27, channels, channels)
    inner_span = inner_dest - span_start
    occupancy_wide = occupancy.astype(jnp.float32)[:, None, :]
    out_features = (jnp.take(out_sum, inner_span, axis=2) * occupancy_wide).astype(jnp.bfloat16)
    in_grad = (jnp.take(back_sum, inner_span, axis=2) * occupancy_wide).astype(jnp.bfloat16)
    grad_scale = float(lax.axis_size("dom") * leaf_count * voxel_count) ** (-0.5)
    summed_grad = lax.psum(grad_local.reshape(-1), "dom")
    weight_grad = summed_grad.reshape(27, channels, channels) * grad_scale
    return (out_features, in_grad, weight_grad)


def solution(mesh):
    placed = (
        P(("scene", "dom"), None, None),
        P(("scene", "dom"), None, None),
        P(),
        P(("scene", "dom"), None),
        P(("scene", "dom"), None),
    )
    return jax.shard_map(
        shards,
        mesh=mesh,
        in_specs=placed,
        out_specs=(
            P(("scene", "dom"), None, None),
            P(("scene", "dom"), None, None),
            P("scene", None, None),
        ),
        check_vma=False,
    )
```

profile of v0, /device:TPU:1, one launch (start us, length us, event | category | flops | bytes accessed | tf_op | source)
XLA Modules:
  0.0 636.6 jit_solution(8888239255000274014)
XLA Ops:
  15.2 5.3 collective-permute-start.1
  87.8 13.8 %scatter_fusion.38 = bf16[8,64,778]{1,0,2:T(8,128)(2,1)S(1)} fusion(bf16[8,64,778]{1,0,2:T(8,128)(2,1)S(1)} %broadcast_in_dim.665, s32[512]{0:T(512)} %constant.642.clone, bf16[512,8,64]{2,1,0:T(8,128)(2,1)S(1)} %bitcast.358), kind=kCustom, calls=%fused_computation.128 | custom fusion | bytes 1574912 | tf_op jit(solution)/shard_map/scatter | solution.py:157
  101.6 2.5 copy.356
  105.8 13.7 %scatter_fusion.19 = bf16[8,64,1000]{1,0,2:T(8,128)(2,1)S(1)} fusion(bf16[8,64,1000]{1,0,2:T(8,128)(2,1)S(1)} %broadcast.489.clone, s32[512]{0:T(512)} %constant.1068, bf16[512,8,64]{2,1,0:T(8,128)(2,1)S(1)} %bitcast.359), kind=kCustom, calls=%fused_computation.109 | custom fusion | bytes 1574912 | tf_op jit(solution)/shard_map/scatter | solution.py:126
  122.1 13.7 %scatter_fusion = bf16[8,64,1000]{1,0,2:T(8,128)(2,1)S(1)} fusion(bf16[8,64,1000]{1,0,2:T(8,128)(2,1)S(1)} %broadcast.489.clone.1, s32[512]{0:T(512)} %constant.1068, bf16[512,8,64]{2,1,0:T(8,128)(2,1)S(1)} %bitcast.361), kind=kCustom, calls=%fused_computation.90 | custom fusion | bytes 1574912 | tf_op jit(solution)/shard_map/scatter | solution.py:126
  249.5 2.7 scatter_fusion.3
  252.2 6.5 %scatter_fusion.22 = bf16[8,64,1000]{1,0,2:T(8,128)(2,1)} fusion(bf16[8,64,1000]{1,0,2:T(8,128)(2,1)} %scatter_fusion.21, s32[64]{0:T(128)S(1)} %copy-done.81, bf16[64,8,64]{2,1,0:T(8,128)(2,1)S(1)} %copy-done.47), kind=kCustom, calls=%fused_computation.112 | custom fusion | bytes 196864 | tf_op jit(solution)/shard_map/scatter | solution.py:149
  268.1 2.6 scatter_fusion.7
  270.7 6.9 %scatter_fusion.26 = bf16[8,64,1000]{1,0,2:T(8,128)(2,1)} fusion(bf16[8,64,1000]{1,0,2:T(8,128)(2,1)} %scatter_fusion.25, s32[64]{0:T(128)S(1)} %copy-done.77, bf16[64,8,64]{2,1,0:T(8,128)(2,1)} %copy.329), kind=kCustom, calls=%fused_computation.116 | custom fusion | bytes 196864 | tf_op jit(solution)/shard_map/scatter | solution.py:149
  280.2 2.4 scatter_fusion.9
  282.7 6.9 %scatter_fusion.28 = bf16[8,64,1000]{1,0,2:T(8,128)(2,1)} fusion(bf16[8,64,1000]{1,0,2:T(8,128)(2,1)} %scatter_fusion.27, s32[64]{0:T(128)S(1)} %copy-done.75, bf16[64,8,64]{2,1,0:T(8,128)(2,1)} %copy.333), kind=kCustom, calls=%fused_computation.118 | custom fusion | bytes 196864 | tf_op jit(solution)/shard_map/scatter | solution.py:149
  289.6 2.4 scatter_fusion.10
  292.1 6.6 %scatter_fusion.29 = bf16[8,64,1000]{1,0,2:T(8,128)(2,1)} fusion(bf16[8,64,1000]{1,0,2:T(8,128)(2,1)} %scatter_fusion.28, s32[64]{0:T(128)S(1)} %copy-done.74, bf16[64,8,64]{2,1,0:T(8,128)(2,1)S(1)} %copy-done.44), kind=kCustom, calls=%fused_computation.119 | custom fusion | bytes 196864 | tf_op jit(solution)/shard_map/scatter | solution.py:149
  303.8 6.6 %scatter_fusion.31 = bf16[8,64,1000]{1,0,2:T(8,128)(2,1)} fusion(bf16[8,64,1000]{1,0,2:T(8,128)(2,1)} %scatter_fusion.30, s32[64]{0:T(128)S(1)} %copy-done.72, bf16[64,8,64]{2,1,0:T(8,128)(2,1)S(1)} %copy-done.42), kind=kCustom, calls=%fused_computation.121 | custom fusion | bytes 196864 | tf_op jit(solution)/shard_map/scatter | solution.py:149
  322.1 6.5 %scatter_fusion.35 = bf16[8,64,1000]{1,0,2:T(8,128)(2,1)} fusion(bf16[8,64,1000]{1,0,2:T(8,128)(2,1)} %scatter_fusion.34, s32[64]{0:T(128)S(1)} %copy-done.68, bf16[64,8,64]{2,1,0:T(8,128)(2,1)S(1)} %copy-done.46), kind=kCustom, calls=%fused_computation.125 | custom fusion | bytes 196864 | tf_op jit(solution)/shard_map/scatter | solution.py:149
  337.1 2.6 copy.355
  339.6 89.4 %while.31 = (s32[]{:T(128)}, f32[8,1,64,778]{3,2,1,0:T(8,128)}, f32[8,1,64,778]{3,2,1,0:T(8,128)}, f32[8,1728,64]{1,2,0:T(8,128)}, bf16[8,1,64,1000]{3,2,1,0:T(8...) while((s32[]{:T(128)}, f32[8,1,64,778]{3,2,1,0:T(8,128)}, ...), condition=%wide.region_56.67_spmd, body=%wide.region_55.66_spmd.sunk | while | flops 516243456 | bytes 22411112 | solution.py:195
  347.0 2.7 fusion.141
  358.2 2.7 fusion.141
  369.3 2.7 fusion.141
  380.4 2.7 fusion.141
  391.5 2.7 fusion.141
  402.7 2.7 fusion.141
  413.8 2.7 fusion.141
  425.0 2.7 fusion.141
  429.0 3.6 copy.357
  432.6 2.8 copy.359
  435.4 4.2 gather_fusion.88
  439.6 2.7 gather_fusion.89
  446.4 2.8 fusion.27
  449.1 2.6 copy.361
  453.3 174.1 %all-reduce.2.cloned.1.call-done = f32[110592]{0:T(1024)} async-done(((f32[110592]{0:T(1024)}), f32[110592]{0:T(1024)}) %all-reduce.2.cloned.1.call-update) | async-done | bytes 442384 | tf_op jit(solution)/shard_map/psum | solution.py:206
  (1058 shorter events, 302.0 us)
Async XLA Ops:
  7.2 620.2 %all-reduce.2.cloned.1.call-start = ((), (), s32[]{:S(2)}) async-start(), calls=%async_computation | async-start | bytes 884736 | tf_op jit(solution)/shard_map/psum | solution.py:206
  15.2 133.5 %collective-permute-start.1 = (bf16[1,2,8,4096]{3,2,1,0:T(8,128)(2,1)}, bf16[1,2,8,4096]{3,2,1,0:T(8,128)(2,1)}, u32[]{:S(2)}, u32[]{:S(2)}) collective-permute-start(bf16[1,2,8,4096]{3,2,1,0:T(8,128)(2,1)} %maximum_bitcast_fusion.1), channel_id=1, source_target_pairs={{1,0},{2,1},{3,2},{4,3},{5,4},{6,5},{7,6},{8,7},{9,8},{10,9},{11,1... | collective-permute-start | bytes 393224 | tf_op jit(solution)/shard_map/ppermute | solution.py:18
  21.9 114.8 %collective-permute-start = (bf16[1,2,8,4096]{3,2,1,0:T(8,128)(2,1)}, bf16[1,2,8,4096]{3,2,1,0:T(8,128)(2,1)}, u32[]{:S(2)}, u32[]{:S(2)}) collective-permute-start(bf16[1,2,8,4096]{3,2,1,0:T(8,128)(2,1)} %maximum_bitcast_fusion), channel_id=1, source_target_pairs={{0,1},{1,2},{2,3},{3,4},{4,5},{5,6},{6,7},{7,8},{8,9},{9,10},{10,1... | collective-permute-start | bytes 393224 | tf_op jit(solution)/shard_map/ppermute | solution.py:17
  48.9 95.8 %copy-start.52 = (s32[1024]{0:T(1024)}, s32[1024]{0:T(1024)S(1)}, u32[]{:S(2)}) copy-start(s32[1024]{0:T(1024)S(1)} %pad_clamp_fusion.38) | copy-start | bytes 12292
  50.1 96.9 %copy-start.53 = (s32[1024]{0:T(1024)}, s32[1024]{0:T(1024)S(1)}, u32[]{:S(2)}) copy-start(s32[1024]{0:T(1024)S(1)} %pad_clamp_fusion.35) | copy-start | bytes 12292
  194.0 31.0 %copy-start.37 = (bf16[16,64,64]{1,0,2:T(8,128)(2,1)S(1)}, bf16[16,64,64]{1,0,2:T(8,128)(2,1)}, u32[]{:S(2)}) copy-start(bf16[16,64,64]{1,0,2:T(8,128)(2,1)} %get-tuple-element.472) | copy-start | bytes 393220
  195.5 30.5 %copy-start.36 = (bf16[16,64,64]{1,0,2:T(8,128)(2,1)S(1)}, bf16[16,64,64]{1,0,2:T(8,128)(2,1)}, u32[]{:S(2)}) copy-start(bf16[16,64,64]{1,0,2:T(8,128)(2,1)} %get-tuple-element.471) | copy-start | bytes 393220
  199.8 29.6 %copy-start.101 = (pred[8]{0:T(512)(128)(4,1)S(1)}, pred[8]{0:T(512)(128)(4,1)}, u32[]{:S(2)}) copy-start(pred[8]{0:T(512)(128)(4,1)} %get-tuple-element.335) | copy-start | bytes 28
  247.4 30.2 %copy-start.28 = (bf16[8,8,64]{2,1,0:T(8,128)(2,1)S(1)}, bf16[8,8,64]{2,1,0:T(8,128)(2,1)}, u32[]{:S(2)}) copy-start(bf16[8,8,64]{2,1,0:T(8,128)(2,1)} %copy.291) | copy-start | bytes 24580
  247.4 30.2 %copy-start.76 = (s32[8]{0:T(128)S(1)}, s32[8]{0:T(128)}, u32[]{:S(2)}) copy-start(s32[8]{0:T(128)} %constant.1076) | copy-start | bytes 100
  259.5 30.1 %copy-start.40 = (bf16[64,8,64]{2,1,0:T(8,128)(2,1)S(1)}, bf16[64,8,64]{2,1,0:T(8,128)(2,1)}, u32[]{:S(2)}) copy-start(bf16[64,8,64]{2,1,0:T(8,128)(2,1)} %copy.295) | copy-start | bytes 196612
  259.5 30.1 %copy-start.74 = (s32[64]{0:T(128)S(1)}, s32[64]{0:T(128)}, u32[]{:S(2)}) copy-start(s32[64]{0:T(128)} %constant.1078) | copy-start | bytes 772
  262.1 30.0 %copy-start.44 = (bf16[64,8,64]{2,1,0:T(8,128)(2,1)S(1)}, bf16[64,8,64]{2,1,0:T(8,128)(2,1)}, u32[]{:S(2)}) copy-start(bf16[64,8,64]{2,1,0:T(8,128)(2,1)} %copy.335) | copy-start | bytes 196612
  262.8 35.8 %copy-start.26 = (bf16[8,8,64]{2,1,0:T(8,128)(2,1)S(1)}, bf16[8,8,64]{2,1,0:T(8,128)(2,1)}, u32[]{:S(2)}) copy-start(bf16[8,8,64]{2,1,0:T(8,128)(2,1)} %copy.297) | copy-start | bytes 24580
  262.8 35.8 %copy-start.73 = (s32[8]{0:T(128)S(1)}, s32[8]{0:T(128)}, u32[]{:S(2)}) copy-start(s32[8]{0:T(128)} %constant.1079) | copy-start | bytes 100
  265.4 34.0 %copy-start.29 = (bf16[8,8,64]{2,1,0:T(8,128)(2,1)S(1)}, bf16[8,8,64]{2,1,0:T(8,128)(2,1)}, u32[]{:S(2)}) copy-start(bf16[8,8,64]{2,1,0:T(8,128)(2,1)} %copy.337) | copy-start | bytes 24580
  266.1 35.1 %copy-start.39 = (bf16[64,8,64]{2,1,0:T(8,128)(2,1)S(1)}, bf16[64,8,64]{2,1,0:T(8,128)(2,1)}, u32[]{:S(2)}) copy-start(bf16[64,8,64]{2,1,0:T(8,128)(2,1)} %copy.299) | copy-start | bytes 196612
  266.2 35.1 %copy-start.72 = (s32[64]{0:T(128)S(1)}, s32[64]{0:T(128)}, u32[]{:S(2)}) copy-start(s32[64]{0:T(128)} %constant.1080) | copy-start | bytes 772
  268.1 35.7 %copy-start.42 = (bf16[64,8,64]{2,1,0:T(8,128)(2,1)S(1)}, bf16[64,8,64]{2,1,0:T(8,128)(2,1)}, u32[]{:S(2)}) copy-start(bf16[64,8,64]{2,1,0:T(8,128)(2,1)} %copy.339) | copy-start | bytes 196612
  270.7 39.7 %copy-start.25 = (bf16[8,8,64]{2,1,0:T(8,128)(2,1)S(1)}, bf16[8,8,64]{2,1,0:T(8,128)(2,1)}, u32[]{:S(2)}) copy-start(bf16[8,8,64]{2,1,0:T(8,128)(2,1)} %copy.301) | copy-start | bytes 24580
  270.7 39.7 %copy-start.71 = (s32[8]{0:T(128)S(1)}, s32[8]{0:T(128)}, u32[]{:S(2)}) copy-start(s32[8]{0:T(128)} %constant.1081) | copy-start | bytes 100
  277.6 33.5 %copy-start.27 = (bf16[8,8,64]{2,1,0:T(8,128)(2,1)S(1)}, bf16[8,8,64]{2,1,0:T(8,128)(2,1)}, u32[]{:S(2)}) copy-start(bf16[8,8,64]{2,1,0:T(8,128)(2,1)} %copy.341) | copy-start | bytes 24580
  278.3 34.7 %copy-start.57 = (bf16[8,64]{1,0:T(8,128)(2,1)S(1)}, bf16[8,64]{1,0:T(8,128)(2,1)}, u32[]{:S(2)}) copy-start(bf16[8,64]{1,0:T(8,128)(2,1)} %gather_fusion.30) | copy-start | bytes 3076
  278.3 34.7 %copy-start.58 = (bf16[8,64]{1,0:T(8,128)(2,1)S(1)}, bf16[8,64]{1,0:T(8,128)(2,1)}, u32[]{:S(2)}) copy-start(bf16[8,64]{1,0:T(8,128)(2,1)} %gather_fusion.74) | copy-start | bytes 3076
  278.3 34.7 %copy-start.91 = (pred[8]{0:T(512)(128)(4,1)S(1)}, pred[8]{0:T(512)(128)(4,1)}, u32[]{:S(2)}) copy-start(pred[8]{0:T(512)(128)(4,1)} %get-tuple-element.339) | copy-start | bytes 28
  278.3 34.7 %copy-start.99 = (pred[8]{0:T(512)(128)(4,1)S(1)}, pred[8]{0:T(512)(128)(4,1)}, u32[]{:S(2)}) copy-start(pred[8]{0:T(512)(128)(4,1)} %get-tuple-element.515) | copy-start | bytes 28
  278.3 35.4 %copy-start.70 = (s32[8]{0:T(128)S(1)}, s32[8]{0:T(128)}, u32[]{:S(2)}) copy-start(s32[8]{0:T(128)} %constant.1082) | copy-start | bytes 100
  282.7 33.7 %copy-start.59 = (bf16[8,64]{1,0:T(8,128)(2,1)S(1)}, bf16[8,64]{1,0:T(8,128)(2,1)}, u32[]{:S(2)}) copy-start(bf16[8,64]{1,0:T(8,128)(2,1)} %gather_fusion.33) | copy-start | bytes 3076
  282.7 33.7 %copy-start.60 = (bf16[8,64]{1,0:T(8,128)(2,1)S(1)}, bf16[8,64]{1,0:T(8,128)(2,1)}, u32[]{:S(2)}) copy-start(bf16[8,64]{1,0:T(8,128)(2,1)} %gather_fusion.77) | copy-start | bytes 3076
  282.7 33.7 %copy-start.90 = (pred[8]{0:T(512)(128)(4,1)S(1)}, pred[8]{0:T(512)(128)(4,1)}, u32[]{:S(2)}) copy-start(pred[8]{0:T(512)(128)(4,1)} %get-tuple-element.337) | copy-start | bytes 28
  282.7 33.6 %copy-start.98 = (pred[8]{0:T(512)(128)(4,1)S(1)}, pred[8]{0:T(512)(128)(4,1)}, u32[]{:S(2)}) copy-start(pred[8]{0:T(512)(128)(4,1)} %get-tuple-element.513) | copy-start | bytes 28
  282.7 34.3 %copy-start.69 = (s32[8]{0:T(128)S(1)}, s32[8]{0:T(128)}, u32[]{:S(2)}) copy-start(s32[8]{0:T(128)} %constant.1083) | copy-start | bytes 100
  (92 other events, 1571.0 us)
Sparse Core Ops, SparseCore 0:
  446.0 181.2 all-reduce.1
where the time goes:
time: 647 us; the launch traced here: 637 us
  local copies, waits for them, and re-layouts  326 us (50%)
  waiting for transfers between devices  174 us (27%)
  other arithmetic  68.5 us (11%)
  matrix products  42.5 us (7%)
  between operations  16.7 us (3%)
  starting transfers between devices  7.22 us (1%)
    psum x1, waiting for transfers between devices, shards(): summed_grad = lax.psum(grad_local.reshape(-1), 'dom')  174 us
    scatter x36, local copies, waits for them, and re-layouts, padded_field(): padded.at[:, :, dest_index].set(take_rows(source, row_index, keep_rows))  87 us
    gather x52, local copies, waits for them, and re-layouts, take_rows(): jnp.take(source, jnp.clip(row_index, 0, source.shape[0] - 1), axis=0)  52.1 us
    while x416, local copies, waits for them, and re-layouts  43.8 us
    scatter x2, local copies, waits for them, and re-layouts, padded_field(): padded = jnp.zeros((leaf_count, channels, padded_cells), center.dtype).at...  27.4 us
    dot_general x8, matrix products, block_terms(): jnp.einsum('lkv,lov->ko', stack_x, dy_block, preferred_element_type=jnp.f...  21.6 us
    select_n x36, local copies, waits for them, and re-layouts, take_rows(): jnp.where(keep_rows[:, None, None], picked, jnp.zeros((), source.dtype))  16.9 us
    gather x40, other arithmetic  15.1 us
  transfers between devices with their start and end apart: 3, of which 1 were waited for; matrix products, arithmetic and copies ran while one was open for 20% of the time, Pallas kernels for 0%

commit v1 on v0

v1 whole, which is shorter than its diff:
```python
import functools

import jax
import jax.numpy as jnp
from jax import lax
from jax.experimental import pallas as pl
from jax.experimental.pallas import tpu as pltpu
from jax.sharding import PartitionSpec as P

LEAVES = 8
CH = 64
SIDE = 8
VOX = 512
PLANE = 64
ROWS = 80
NY = 4
TILES = 14
MESH = pl.DeviceIdType.MESH
F32 = jnp.float32
BF16 = jnp.bfloat16


def tap(p, q, r):
    return 9 * (p + 1) + 3 * (q + 1) + r + 1


def copy_to(src, dst, send, recv, dom):
    return pltpu.make_async_remote_copy(
        src_ref=src,
        dst_ref=dst,
        send_sem=send,
        recv_sem=recv,
        device_id={"dom": dom},
        device_id_type=MESH,
    )


def kernel(
    nz,
    scale,
    x_ref,
    dy_ref,
    w_ref,
    words_ref,
    near_ref,
    out_ref,
    back_ref,
    grad_ref,
    occ,
    xd,
    high,
    low,
    send_high,
    send_low,
    got_high,
    got_low,
    a0,
    a1,
    a2,
    zt,
    wf,
    wb,
    g,
    part,
    r1,
    u,
    r2,
    v,
    r3,
    own,
    f3,
    full,
    halo_sems,
    core_sems,
    y_sems,
    z_sems,
):
    ndom = nz * 8
    dom = lax.axis_index("dom")
    core = lax.rem(dom, 2)
    y = lax.rem(lax.div(dom, 2), NY)
    z = lax.div(dom, 8)
    up = lax.rem(dom + 1, ndom)
    down = lax.rem(dom + ndom - 1, ndom)
    mate = z * 8 + y * 2 + (1 - core)
    y_mates = [z * 8 + lax.rem(y + k, NY) * 2 + core for k in range(1, NY)]
    z_mates = [lax.rem(z + k, nz) * 8 + y * 2 + core for k in range(1, nz)]

    barrier = pltpu.get_barrier_semaphore()
    partners = [up, down, mate] + y_mates + z_mates
    for d in partners:
        pl.semaphore_signal(barrier, inc=1, device_id={"dom": d}, device_id_type=MESH)

    at = lax.broadcasted_iota(jnp.int32, (LEAVES, VOX), 1)
    word_at = lax.shift_right_logical(at * 2185, 16)
    bit_at = at - 30 * word_at
    words = jnp.zeros((LEAVES, VOX), jnp.int32)
    for n in range(18):
        words = jnp.where(word_at == n, words_ref[:, n : n + 1], words)
    bits = (lax.shift_right_logical(words, bit_at) & 1).astype(F32)
    for s in range(LEAVES):
        occ[s] = bits[s : s + 1]

    def prepare(s, carry):
        both = jnp.concatenate([x_ref[s].astype(F32), dy_ref[s].astype(F32)], axis=0)
        turned = (both * occ[s]).T.reshape(SIDE, SIDE, SIDE, 128)
        xd[s] = turned
        high[s] = turned[SIDE - 1]
        low[s] = turned[0]
        send_high[s] = turned[SIDE - 1].reshape(PLANE, 128).astype(BF16)
        send_low[s] = turned[0].reshape(PLANE, 128).astype(BF16)
        return carry

    lax.fori_loop(0, LEAVES, prepare, 0)
    xd[LEAVES] = jnp.zeros((SIDE, SIDE, SIDE, 128), F32)
    high[2 * LEAVES] = jnp.zeros((SIDE, SIDE, 128), F32)
    low[2 * LEAVES] = jnp.zeros((SIDE, SIDE, 128), F32)

    pl.semaphore_wait(barrier, len(partners))
    copy_up = copy_to(send_high, got_high, halo_sems.at[0, 0], halo_sems.at[0, 1], up)
    copy_down = copy_to(send_low, got_low, halo_sems.at[1, 0], halo_sems.at[1, 1], down)
    copy_up.start()
    copy_down.start()

    none = jnp.zeros((CH, CH), F32)

    def weight(p, q, r):
        return w_ref[tap(p, q, r)].astype(F32)

    for n, p in enumerate((-1, 0, 1)):
        rows = []
        for r in (-1, 0, 1):
            rows.append(
                jnp.concatenate([weight(p, -1, r), weight(p, 0, r), weight(p, 1, r), none], axis=1)
            )
        rows.append(jnp.zeros((CH, 4 * CH), F32))
        wf[n * 256 : (n + 1) * 256] = jnp.concatenate(rows, axis=0).astype(BF16)
        cols = []
        for q in (0, -1, None, 1):
            if q is None:
                cols.append(jnp.zeros((CH, 4 * CH), F32))
            else:
                cols.append(
                    jnp.concatenate(
                        [weight(-p, -q, 0), weight(-p, -q, 1), none, weight(-p, -q, -1)], axis=1
                    )
                )
        wb[n * 256 : (n + 1) * 256] = jnp.concatenate(cols, axis=0).T.astype(BF16)

    sub = lax.broadcasted_iota(jnp.int32, (10, SIDE, 128), 1)
    lane = lax.broadcasted_iota(jnp.int32, (10, SIDE, 128), 2)
    left = lane < CH
    first, last = sub == 0, sub == SIDE - 1

    def source(s, p, q, r):
        t = tap(p, q, r)
        if t == 13:
            return s
        n = near_ref[s, t if t < 13 else t - 1]
        slot = n & 7
        if p == 0:
            return jnp.where(n < 0, LEAVES, slot)
        here = lax.shift_right_arithmetic(n, 3) == dom
        return jnp.where(n < 0, 2 * LEAVES, jnp.where(here, slot, LEAVES + slot))

    def build(s, row, pool, ids):
        def line(r):
            return jnp.concatenate(
                [pool(ids[0, r], SIDE - 1, SIDE), pool(ids[1, r], 0, SIDE), pool(ids[2, r], 0, 1)],
                axis=0,
            )

        mid, before, after = line(1), line(0), line(2)
        less = pltpu.roll(jnp.where(last, before, mid), 1, 1)
        more = pltpu.roll(jnp.where(first, after, mid), SIDE - 1, 1)
        swapped = pltpu.roll(mid, CH, 2)
        a0[s, row] = jnp.where(left, less, swapped).reshape(ROWS, 128).astype(BF16)
        a1[s, row] = jnp.where(left, swapped, less).reshape(ROWS, 128).astype(BF16)
        a2[s, row] = more.reshape(ROWS, 128).astype(BF16)

    def inner(s, carry):
        ids = {(q + 1, r + 1): source(s, 0, q, r) for q in (-1, 0, 1) for r in (-1, 0, 1)}
        for a in range(SIDE):
            build(s, a + 1, lambda i, lo, hi, a=a: xd[i, a, lo:hi], ids)
        mine = xd[s]
        gap = jnp.zeros((SIDE, 1, SIDE, 128), F32)
        below = jnp.concatenate([mine, gap, gap], axis=1).reshape(SIDE * ROWS, 128)
        same = jnp.concatenate([gap, mine, gap], axis=1).reshape(SIDE * ROWS, 128)
        above = jnp.concatenate([gap, gap, mine], axis=1).reshape(SIDE * ROWS, 128)
        cols = pl.ds(pl.multiple_of(s * (SIDE * ROWS), 128), SIDE * ROWS)
        zt[0:CH, cols] = below.T[CH:].astype(BF16)
        zt[CH : 2 * CH, cols] = same.T[CH:].astype(BF16)
        zt[2 * CH :, cols] = above.T[CH:].astype(BF16)
        return carry

    lax.fori_loop(0, LEAVES, inner, 0)

    copy_up.wait()
    copy_down.wait()
    for s in range(LEAVES):
        high[LEAVES + s] = got_high[s].astype(F32).reshape(SIDE, SIDE, 128)
        low[LEAVES + s] = got_low[s].astype(F32).reshape(SIDE, SIDE, 128)

    def outer(s, carry):
        for p, row, pool in ((-1, 0, high), (1, SIDE + 1, low)):
            ids = {(q + 1, r + 1): source(s, p, q, r) for q in (-1, 0, 1) for r in (-1, 0, 1)}
            build(s, row, lambda i, lo, hi, pool=pool: pool[i, lo:hi], ids)
        return carry

    lax.fori_loop(0, LEAVES, outer, 0)

    for n in range(3):

        def term(h, total, n=n):
            cols = pl.ds(pl.multiple_of(h * (2 * SIDE * ROWS), 128), 2 * SIDE * ROWS)
            rows = pl.ds(h * 2, 2)
            right = jnp.concatenate(
                [
                    a0[rows, n : n + SIDE].reshape(2 * SIDE * ROWS, 128),
                    a2[rows, n : n + SIDE].reshape(2 * SIDE * ROWS, 128),
                ],
                axis=1,
            )
            return total + jnp.dot(zt[:, cols], right, preferred_element_type=F32)

        total = lax.fori_loop(0, LEAVES // 2, term, jnp.zeros((3 * CH, 256), F32))
        g[n] = total.T

    def put(index, value):
        part[index // TILES, index % TILES] = value

    for j in range(9):
        for k in range(8):
            at_row = (j % 3) * CH + 8 * k
            put(8 * j + k, g[j // 3, at_row : at_row + 8, 0:128])
    for j in range(5):
        lower = g[j // 3, (j % 3) * CH : (j % 3 + 1) * CH, 128:192]
        if j < 4:
            m = j + 5
            upper = g[m // 3, (m % 3) * CH : (m % 3 + 1) * CH, 128:192]
        else:
            upper = none
        pair = jnp.concatenate([lower, upper], axis=1)
        for k in range(8):
            put(72 + 8 * j + k, pair[8 * k : 8 * k + 8])

    half = lax.broadcasted_iota(jnp.int32, (SIDE * ROWS, 128), 1) < CH

    def convolve(s, carry):
        xs, ds = [], []
        for n in range(3):
            one = a0[s, n : n + SIDE].reshape(SIDE * ROWS, 128)
            two = a1[s, n : n + SIDE].reshape(SIDE * ROWS, 128)
            three = a2[s, n : n + SIDE].reshape(SIDE * ROWS, 128)
            xs += [one, three]
            ds += [two, three]
        yo = jnp.dot(jnp.concatenate(xs, axis=1), wf[...], preferred_element_type=F32)
        yb = jnp.dot(jnp.concatenate(ds, axis=1), wb[...], preferred_element_type=F32)
        shape = (SIDE, 10, SIDE, 128)
        ahead = (yo[:, 128:] + yb[:, 128:]).reshape(shape)
        behind = jnp.where(half, yo[:, :128], yb[:, :128]).reshape(shape)
        level = pltpu.roll(jnp.where(half, yb[:, :128], yo[:, :128]), CH, 1).reshape(shape)
        total = behind[:, 0:8] + level[:, 1:9] + ahead[:, 2:10]
        turned = total.reshape(VOX, 128).T * occ[s]
        out_ref[s] = turned[:CH].astype(BF16)
        back_ref[s] = turned[CH:].astype(BF16)
        return carry

    theirs, ours = pl.ds((1 - core) * NY, NY), pl.ds(core * NY, NY)
    c1 = copy_to(part.at[theirs], r1, core_sems.at[0, 0], core_sems.at[0, 1], mate)
    c1.start()
    lax.fori_loop(0, 1, convolve, 0)
    c1.wait()
    for k in range(NY):
        u[k] = part[core * NY + k] + r1[k]
    c2 = [
        copy_to(
            u.at[lax.rem(y + k, NY)], r2.at[k - 1], y_sems.at[0, k - 1], y_sems.at[1, k - 1], y_mates[k - 1]
        )
        for k in range(1, NY)
    ]
    for c in c2:
        c.start()
    lax.fori_loop(1, 3, convolve, 0)
    for c in c2:
        c.wait()
    v[0:TILES] = u[y] + r2[0] + r2[1] + r2[2]
    v[TILES:] = jnp.zeros((16 - TILES, 8, 128), F32)
    per = 16 // nz
    c3 = [
        copy_to(
            v.at[pl.ds(lax.rem(z + k, nz) * per, per)],
            r3.at[k - 1],
            z_sems.at[0, k - 1],
            z_sems.at[1, k - 1],
            z_mates[k - 1],
        )
        for k in range(1, nz)
    ]
    for c in c3:
        c.start()
    lax.fori_loop(3, 4, convolve, 0)
    for c in c3:
        c.wait()
    mine = v[pl.ds(z * per, per)]
    for k in range(nz - 1):
        mine = mine + r3[k]
    own[...] = mine * scale
    c4 = [
        copy_to(
            own, f3.at[pl.ds(z * per, per)], z_sems.at[2, k - 1], z_sems.at[3, k - 1], z_mates[k - 1]
        )
        for k in range(1, nz)
    ]
    for c in c4:
        c.start()
    f3[pl.ds(z * per, per)] = own[...]
    lax.fori_loop(4, 5, convolve, 0)
    for c in c4:
        c.wait()
    c5 = [
        copy_to(
            f3.at[pl.ds(0, TILES)],
            full.at[core * NY + y],
            y_sems.at[2, k - 1],
            y_sems.at[3, k - 1],
            y_mates[k - 1],
        )
        for k in range(1, NY)
    ]
    for c in c5:
        c.start()
    full[core * NY + y] = f3[0:TILES]
    lax.fori_loop(5, 7, convolve, 0)
    for c in c5:
        c.wait()
    c6 = copy_to(full.at[ours], full.at[ours], core_sems.at[1, 0], core_sems.at[1, 1], mate)
    c6.start()
    lax.fori_loop(7, 8, convolve, 0)
    c6.wait()

    def tile(index):
        return full[index // TILES, index % TILES]

    for j in range(9):
        p, r = j // 3 - 1, j % 3 - 1
        for k in range(8):
            rows = slice(8 * k, 8 * k + 8)
            value = tile(8 * j + k)
            grad_ref[tap(p, -1, r), rows] = value[:, :CH]
            grad_ref[tap(p, 0, r), rows] = value[:, CH:]
            m = j if j < 5 else j - 5
            value = tile(72 + 8 * m + k)
            grad_ref[tap(p, 1, r), rows] = value[:, :CH] if j < 5 else value[:, CH:]


def shards(nz, features, cotangent, weight, mask_words, neighbors):
    scale = float(nz * 8 * LEAVES * VOX) ** -0.5
    vmem = pltpu.VMEM
    per = 16 // nz
    dma = pltpu.SemaphoreType.DMA
    any_vmem = pl.BlockSpec(memory_space=pltpu.VMEM)
    field = jax.ShapeDtypeStruct((LEAVES, CH, VOX), BF16)
    return pl.pallas_call(
        functools.partial(kernel, nz, scale),
        out_shape=(field, field, jax.ShapeDtypeStruct((27, CH, CH), F32)),
        in_specs=[any_vmem] * 4 + [pl.BlockSpec(memory_space=pltpu.SMEM)],
        out_specs=(any_vmem,) * 3,
        scratch_shapes=[
            vmem((LEAVES, 1, VOX), F32),
            vmem((LEAVES + 1, SIDE, SIDE, SIDE, 128), F32),
            vmem((2 * LEAVES + 1, SIDE, SIDE, 128), F32),
            vmem((2 * LEAVES + 1, SIDE, SIDE, 128), F32),
            vmem((LEAVES, PLANE, 128), BF16),
            vmem((LEAVES, PLANE, 128), BF16),
            vmem((LEAVES, PLANE, 128), BF16),
            vmem((LEAVES, PLANE, 128), BF16),
            vmem((LEAVES, 10, ROWS, 128), BF16),
            vmem((LEAVES, 10, ROWS, 128), BF16),
            vmem((LEAVES, 10, ROWS, 128), BF16),
            vmem((3 * CH, LEAVES * SIDE * ROWS), BF16),
            vmem((768, 256), BF16),
            vmem((768, 256), BF16),
            vmem((3, 256, 192), F32),
            vmem((8, TILES, 8, 128), F32),
            vmem((NY, TILES, 8, 128), F32),
            vmem((NY, TILES, 8, 128), F32),
            vmem((NY - 1, TILES, 8, 128), F32),
            vmem((16, 8, 128), F32),
            vmem((nz - 1, per, 8, 128), F32),
            vmem((per, 8, 128), F32),
            vmem((16, 8, 128), F32),
            vmem((8, TILES, 8, 128), F32),
            dma((2, 2)),
            dma((2, 2)),
            dma((4, NY - 1)),
            dma((4, nz - 1)),
        ],
        compiler_params=pltpu.CompilerParams(
            collective_id=0, has_side_effects=True, vmem_limit_bytes=48 * 2**20
        ),
        name="sparse_conv",
    )(features, cotangent, weight, mask_words, neighbors)


def solution(mesh):
    placed = (
        P(("scene", "dom"), None, None),
        P(("scene", "dom"), None, None),
        P(),
        P(("scene", "dom"), None),
        P(("scene", "dom"), None),
    )
    return jax.shard_map(
        functools.partial(shards, mesh.shape["dom"] // 8),
        mesh=mesh,
        in_specs=placed,
        out_specs=(
            P(("scene", "dom"), None, None),
            P(("scene", "dom"), None, None),
            P("scene", None, None),
        ),
        check_vma=False,
    )
```

time: 647 us -> 50.1 us (0.08); the launches traced: 637 us -> 49.9 us
  local copies, waits for them, and re-layouts: 326 us -> 6.96 us
  waiting for transfers between devices: 174 us -> 0 us
  other arithmetic: 68.5 us -> 0 us
  matrix products: 42.5 us -> 0 us
  Pallas kernels: 0 us -> 42.3 us
  between operations: 16.7 us -> 0.65 us
  starting transfers between devices: 7.22 us -> 0 us
    psum x1 -> x0, waiting for transfers between devices: 174 us -> none  [shards(): summed_grad = lax.psum(grad_local.reshape(-1), 'dom')]
    scatter x39 -> x0, local copies, waits for them, and re-layouts: 128 us -> none  [the longest x36 87 us: padded_field(): padded.at[:, :, dest_index].set(take_rows(source, row_index, keep_rows))]
    gather x110 -> x0, local copies, waits for them, and re-layouts: 92.4 us -> none  [the longest x52 52.1 us: take_rows(): jnp.take(source, jnp.clip(row_index, 0, source.shape[0] - 1), axis=0)]
    while x421 -> x0, local copies, waits for them, and re-layouts: 57.3 us -> none
    dot_general x24 -> x0, matrix products: 42.5 us -> none  [the longest x8 21.6 us: block_terms(): jnp.einsum('lkv,lov->ko', stack_x, dy_block, preferred_element_type=jnp.f...]
    pallas_call x0 -> x1, Pallas kernels: none -> 42.3 us  [shards(): pl.pallas_call(functools.partial(kernel, nz, scale), out_shape=(field, fi...]
    select_n x52 -> x0, local copies, waits for them, and re-layouts: 21.7 us -> none  [the longest x36 16.9 us: take_rows(): jnp.where(keep_rows[:, None, None], picked, jnp.zeros((), source.dtype))]
    select_n x38 -> x0, other arithmetic: 18.2 us -> none  [the longest x18 10.6 us: take_rows(): jnp.where(keep_rows[:, None, None], picked, jnp.zeros((), source.dtype))]
  transfers between devices with their start and end apart: 3 -> 0, of which waited for: 1 -> 0; matrix products, arithmetic and copies ran while one was open for 20% -> 0% of each run, Pallas kernels for 0% -> 0%
where the time goes in v1:
time: 50.1 us; the launch traced here: 49.9 us
  Pallas kernels  42.3 us (84%)
  local copies, waits for them, and re-layouts  6.96 us (14%)
  between operations  0.65 us (1%)
    pallas_call x1, Pallas kernels, shards(): pl.pallas_call(functools.partial(kernel, nz, scale), out_shape=(field, fi...  42.3 us
    unnamed x13, local copies, waits for them, and re-layouts  6.96 us

profile of v1, /device:TPU:1, one launch (start us, length us, event | category | flops | bytes accessed | tf_op | source)
XLA Modules:
  0.0 49.9 jit_solution(2915161225849965610)
XLA Ops:
  0.6 0.0 copy-start
  0.6 1.0 %copy-done = bf16[8,64,512]{2,1,0:T(8,128)(2,1)S(1)} copy-done((bf16[8,64,512]{2,1,0:T(8,128)(2,1)S(1)}, bf16[8,64,512]{2,1,0:T(8,128)(2,1)}, u32[]{:S(2)}) %copy-start) | copy-done | bytes 524312
  1.7 0.0 copy-start.1
  1.7 1.0 %copy-done.1 = bf16[8,64,512]{2,1,0:T(8,128)(2,1)S(1)} copy-done((bf16[8,64,512]{2,1,0:T(8,128)(2,1)S(1)}, bf16[8,64,512]{2,1,0:T(8,128)(2,1)}, u32[]{:S(2)}) %copy-start.1) | copy-done | bytes 524312
  2.7 0.0 copy-start.2
  2.7 1.0 %copy-done.2 = bf16[27,64,64]{2,1,0:T(8,128)(2,1)S(1)} copy-done((bf16[27,64,64]{2,1,0:T(8,128)(2,1)S(1)}, bf16[27,64,64]{2,1,0:T(8,128)(2,1)}, u32[]{:S(2)}) %copy-start.2) | copy-done | bytes 221208
  3.7 0.0 copy-start.3
  3.7 0.7 %copy-done.3 = s32[8,18]{1,0:T(8,128)S(1)} copy-done((s32[8,18]{1,0:T(8,128)S(1)}, s32[8,18]{1,0:T(8,128)}, u32[]{:S(2)}) %copy-start.3) | copy-done | bytes 600
  4.4 0.0 copy-start.4
  4.4 0.7 %copy-done.4 = s32[8,26]{1,0:T(8,128)S(1)} copy-done((s32[8,26]{1,0:T(8,128)S(1)}, s32[8,26]{1,0:T(8,128)}, u32[]{:S(2)}) %copy-start.4) | copy-done | bytes 856
  5.1 42.3 %sparse_conv.1 = (bf16[8,64,512]{2,1,0:T(8,128)(2,1)S(1)}, bf16[8,64,512]{2,1,0:T(8,128)(2,1)S(1)}, f32[27,64,64]{2,1,0:T(8,128)S(1)}) custom-call(bf16[8,64,512]{2,1,0:T(8,128)(2,1)S(1)} %copy-done, bf16[8,64,512]{2,1,0:T(8,128)(2,1)S(1)} %copy-done.1, bf16[27,64,64]{2,1,0:T(8,128)(2,1)S(1)} %copy-done.2, s32[8,18]{1,0:T(8,128)S(1)} %copy-done.3, ...), custom_call_target="tpu_custom_call" | custom-call | tf_op jit(solution)/shard_map/sparse_conv/pallas_call | solution.py:364
  47.4 0.8 %copy.11 = bf16[8,64,512]{2,1,0:T(8,128)(2,1)} copy(bf16[8,64,512]{2,1,0:T(8,128)(2,1)S(1)} %get-tuple-element.6) | data formatting | bytes 1048576
  48.2 0.8 %copy.12 = bf16[8,64,512]{2,1,0:T(8,128)(2,1)} copy(bf16[8,64,512]{2,1,0:T(8,128)(2,1)S(1)} %get-tuple-element.7) | data formatting | bytes 1048576
  49.0 0.9 %copy.13 = f32[27,64,64]{2,1,0:T(8,128)} copy(f32[27,64,64]{2,1,0:T(8,128)S(1)} %get-tuple-element.8) | data formatting | bytes 884736
Async XLA Ops:
  0.6 1.0 %copy-start = (bf16[8,64,512]{2,1,0:T(8,128)(2,1)S(1)}, bf16[8,64,512]{2,1,0:T(8,128)(2,1)}, u32[]{:S(2)}) copy-start(bf16[8,64,512]{2,1,0:T(8,128)(2,1)} %x_ref.1) | copy-start | bytes 1572868
  1.7 1.0 %copy-start.1 = (bf16[8,64,512]{2,1,0:T(8,128)(2,1)S(1)}, bf16[8,64,512]{2,1,0:T(8,128)(2,1)}, u32[]{:S(2)}) copy-start(bf16[8,64,512]{2,1,0:T(8,128)(2,1)} %dy_ref.1) | copy-start | bytes 1572868
  2.7 1.0 %copy-start.2 = (bf16[27,64,64]{2,1,0:T(8,128)(2,1)S(1)}, bf16[27,64,64]{2,1,0:T(8,128)(2,1)}, u32[]{:S(2)}) copy-start(bf16[27,64,64]{2,1,0:T(8,128)(2,1)} %w_ref.1) | copy-start | bytes 663556
  3.7 0.7 %copy-start.3 = (s32[8,18]{1,0:T(8,128)S(1)}, s32[8,18]{1,0:T(8,128)}, u32[]{:S(2)}) copy-start(s32[8,18]{1,0:T(8,128)} %words_ref.1) | copy-start | bytes 1732
  4.4 0.7 %copy-start.4 = (s32[8,26]{1,0:T(8,128)S(1)}, s32[8,26]{1,0:T(8,128)}, u32[]{:S(2)}) copy-start(s32[8,26]{1,0:T(8,128)} %near_ref.1) | copy-start | bytes 2500

commit v2 on v1

v2 whole, which is shorter than its diff:
```python
import functools

import jax
import jax.numpy as jnp
from jax import lax
from jax.experimental import pallas as pl
from jax.experimental.pallas import tpu as pltpu
from jax.sharding import PartitionSpec as P

LEAVES = 8
CH = 64
SIDE = 8
VOX = 512
PLANE = 64
ROWS = 80
WIDE = 640
MESH = pl.DeviceIdType.MESH
F32 = jnp.float32
BF16 = jnp.bfloat16


def tap(p, q, r):
    return 9 * (p + 1) + 3 * (q + 1) + r + 1


def copy_to(src, dst, send, recv, dom):
    return pltpu.make_async_remote_copy(
        src_ref=src,
        dst_ref=dst,
        send_sem=send,
        recv_sem=recv,
        device_id={"dom": dom},
        device_id_type=MESH,
    )


def kernel(
    cells,
    scale,
    x_hbm,
    dy_hbm,
    w_hbm,
    words_hbm,
    near_hbm,
    out_hbm,
    back_hbm,
    grad_hbm,
    out_ref,
    back_ref,
    grad_ref,
    x_ref,
    dy_ref,
    w_ref,
    words_ref,
    near_ref,
    occ,
    xd,
    high,
    low,
    send_high,
    send_low,
    got_high,
    got_low,
    a0,
    a1,
    a2,
    zt,
    wf,
    wb,
    g,
    sums,
    part,
    mates,
    summed,
    terms,
    own,
    full,
    in_sems,
    out_sems,
    halo_sems,
    core_sems,
    scatter_sent,
    scatter_got,
    gather_sent,
    gather_got,
):
    ndom = cells * 2
    dom = lax.axis_index("dom")
    core = lax.rem(dom, 2)
    cell = lax.div(dom, 2)
    up = lax.rem(dom + 1, ndom)
    down = lax.rem(dom + ndom - 1, ndom)
    mate = dom + 1 - 2 * core
    groups, per = part.shape[2:4]
    middle = cells // 2 + 2

    fetches = [
        pltpu.make_async_copy(source, dest, in_sems.at[n])
        for n, (source, dest) in enumerate(
            (
                (words_hbm, words_ref),
                (x_hbm, x_ref),
                (dy_hbm, dy_ref),
                (near_hbm, near_ref),
                (w_hbm, w_ref),
            )
        )
    ]
    for fetch in fetches:
        fetch.start()

    barrier = pltpu.get_barrier_semaphore()

    def greet(k, carry):
        to = lax.rem(cell + k, cells) * 2 + core
        pl.semaphore_signal(barrier, inc=1, device_id={"dom": to}, device_id_type=MESH)
        return carry

    for d in (up, down, mate):
        pl.semaphore_signal(barrier, inc=1, device_id={"dom": d}, device_id_type=MESH)
    lax.fori_loop(1, cells, greet, 0)
    fetches[0].wait()

    at = lax.broadcasted_iota(jnp.int32, (LEAVES, VOX), 1)
    word_at = lax.shift_right_logical(at * 2185, 16)
    bit_at = at - 30 * word_at
    words = jnp.zeros((LEAVES, VOX), jnp.int32)
    for n in range(18):
        words = jnp.where(word_at == n, words_ref[:, n : n + 1], words)
    bits = (lax.shift_right_logical(words, bit_at) & 1).astype(F32)
    for s in range(LEAVES):
        occ[s] = bits[s : s + 1]

    def prepare(s, carry):
        both = jnp.concatenate([x_ref[s].astype(F32), dy_ref[s].astype(F32)], axis=0)
        turned = (both * occ[s]).T.reshape(SIDE, SIDE, SIDE, 128)
        xd[s] = turned
        high[s] = turned[SIDE - 1]
        low[s] = turned[0]
        send_high[s] = turned[SIDE - 1].reshape(PLANE, 128).astype(BF16)
        send_low[s] = turned[0].reshape(PLANE, 128).astype(BF16)
        return carry

    fetches[1].wait()
    fetches[2].wait()
    lax.fori_loop(0, LEAVES, prepare, 0)
    xd[LEAVES] = jnp.zeros((SIDE, SIDE, SIDE, 128), F32)
    high[2 * LEAVES] = jnp.zeros((SIDE, SIDE, 128), F32)
    low[2 * LEAVES] = jnp.zeros((SIDE, SIDE, 128), F32)

    pl.semaphore_wait(barrier, cells + 2)
    copy_up = copy_to(send_high, got_high, halo_sems.at[0, 0], halo_sems.at[0, 1], up)
    copy_down = copy_to(send_low, got_low, halo_sems.at[1, 0], halo_sems.at[1, 1], down)
    copy_up.start()
    copy_down.start()

    none = jnp.zeros((CH, CH), F32)
    sub = lax.broadcasted_iota(jnp.int32, (10, SIDE, 128), 1)
    lane = lax.broadcasted_iota(jnp.int32, (10, SIDE, 128), 2)
    left = lane < CH
    first, last = sub == 0, sub == SIDE - 1

    def source(s, p, q, r):
        t = tap(p, q, r)
        if t == 13:
            return s
        n = near_ref[s, t if t < 13 else t - 1]
        slot = n & 7
        if p == 0:
            return jnp.where(n < 0, LEAVES, slot)
        here = lax.shift_right_arithmetic(n, 3) == dom
        return jnp.where(n < 0, 2 * LEAVES, jnp.where(here, slot, LEAVES + slot))

    def build(s, row, pool, ids):
        def line(r):
            return jnp.concatenate(
                [pool(ids[0, r], SIDE - 1, SIDE), pool(ids[1, r], 0, SIDE), pool(ids[2, r], 0, 1)],
                axis=0,
            )

        mid, before, after = line(1), line(0), line(2)
        less = pltpu.roll(jnp.where(last, before, mid), 1, 1)
        more = pltpu.roll(jnp.where(first, after, mid), SIDE - 1, 1)
        swapped = pltpu.roll(mid, CH, 2)
        a0[row, s] = jnp.where(left, less, swapped).reshape(ROWS, 128).astype(BF16)
        a1[row, s] = jnp.where(left, swapped, less).reshape(ROWS, 128).astype(BF16)
        a2[row, s] = more.reshape(ROWS, 128).astype(BF16)

    def inner(s, carry):
        ids = {(q + 1, r + 1): source(s, 0, q, r) for q in (-1, 0, 1) for r in (-1, 0, 1)}
        for a in range(SIDE):
            build(s, a + 1, lambda i, lo, hi, a=a: xd[i, a, lo:hi], ids)
        return carry

    gap = jnp.zeros((LEAVES, 1, SIDE, 128), F32)

    def spread(field, q):
        parts = [gap, gap]
        parts.insert(q + 1, field)
        return jnp.concatenate(parts, axis=1).reshape(WIDE, 128)

    def turn(h, carry):
        a, b = 2 * h, 2 * h + 1
        one, two = xd[0:LEAVES, a], xd[0:LEAVES, b]
        cols = [pl.ds(pl.multiple_of(plane * WIDE, 128), WIDE) for plane in (a, b)]
        side = lax.broadcasted_iota(jnp.int32, (WIDE, 128), 1) < CH
        rolled = [pltpu.roll(one, CH, 3), pltpu.roll(two, CH, 3)]
        for n, field in enumerate((one, two)):
            both = jnp.where(side, spread(rolled[n], -1), spread(field, 0))
            zt[0 : 2 * CH, cols[n]] = both.astype(BF16).T
        both = jnp.where(side, spread(rolled[0], 1), spread(two, 1)).astype(BF16).T
        zt[2 * CH :, cols[0]] = both[:CH]
        zt[2 * CH :, cols[1]] = both[CH:]
        return carry

    def planes(p, a, count):
        right = jnp.concatenate(
            [
                a0[pl.ds(a + p + 1, count)].reshape(count * WIDE, 128),
                a2[pl.ds(a + p + 1, count)].reshape(count * WIDE, 128),
            ],
            axis=1,
        )
        cols = pl.ds(pl.multiple_of(a * WIDE, 128), count * WIDE)
        return jnp.dot(zt[:, cols], right, preferred_element_type=F32)

    def gradient(n, p, start, pairs):
        total = lax.fori_loop(
            0,
            pairs,
            lambda h, t: t + planes(p, start + 2 * h, 2),
            jnp.zeros((3 * CH, 256), F32),
        )
        if pairs < 4:
            total = total + planes(p, start + 2 * pairs, 1)
        sums[n] = total

    def lay(n):
        g[...] = sums[n].T

        def put(t, value):
            part[n, t // 18, t % 18 // per, t % 18 % per] = value

        for t in range(24):
            put(t, g[8 * t : 8 * t + 8, 0:128])
        ahead = jnp.concatenate([g[0:CH, 128:], g[CH : 2 * CH, 128:]], axis=1)
        for t in range(8):
            put(24 + t, ahead[8 * t : 8 * t + 8])
        ahead = jnp.concatenate([g[2 * CH : 160, 128:], g[160:192, 128:]], axis=1)
        for t in range(4):
            put(32 + t, ahead[8 * t : 8 * t + 8])

    def give(n, p):
        for t in range(36):
            value = full[n, t // 18, t % 18 // per, t % 18 % per]
            if t < 24:
                r, rows = t // 8 - 1, slice(t % 8 * 8, t % 8 * 8 + 8)
                grad_ref[tap(p, -1, r), rows] = value[:, :CH]
                grad_ref[tap(p, 0, r), rows] = value[:, CH:]
            elif t < 32:
                rows = slice((t - 24) * 8, (t - 24) * 8 + 8)
                grad_ref[tap(p, 1, -1), rows] = value[:, :CH]
                grad_ref[tap(p, 1, 0), rows] = value[:, CH:]
            else:
                at_row = (t - 32) * 8
                grad_ref[tap(p, 1, 1), at_row : at_row + 8] = value[:, :CH]
                grad_ref[tap(p, 1, 1), 32 + at_row : 40 + at_row] = value[:, CH:]

    def pair(n):
        return copy_to(part.at[n, 1 - core], mates.at[n], core_sems.at[0, n], core_sems.at[1, n], mate)

    def pair_back(n):
        whole = full.at[n, core]
        return copy_to(whole, whole, core_sems.at[2, n], core_sems.at[3, n], mate)

    def scatter(n, to, j):
        k = lax.rem(to - cell + cells, cells)
        return copy_to(
            summed.at[n, j], terms.at[n, k], scatter_sent.at[n], scatter_got.at[n], to * 2 + core
        )

    def gather(n, k, j):
        to = lax.rem(cell + k, cells)
        return copy_to(
            own.at[n], full.at[n, core, j], gather_sent.at[n], gather_got.at[n], to * 2 + core
        )

    def whole(ref, sent, got):
        return copy_to(ref, ref, sent, got, mate)

    def owning(n, do):
        j = mine(n)

        @pl.when(j < groups)
        def _():
            do(True, j)

        @pl.when(j >= groups)
        def _():
            do(False, j)

    def scatter_sent_wait(n):
        def do(owns, j):
            ref = summed.at[n, pl.ds(0, groups - owns)]
            whole(ref, scatter_sent.at[n], scatter_got.at[n]).wait_send()

        owning(n, do)

    def gather_got_wait(n):
        def do(owns, j):
            ref = full.at[n, core, pl.ds(0, groups - owns)]
            whole(ref, gather_sent.at[n], gather_got.at[n]).wait_recv()

        owning(n, do)

    def gather_sent_wait(n):
        @pl.when(mine(n) < groups)
        def _():
            ref = terms.at[n, pl.ds(1, cells - 1)]
            whole(ref, gather_sent.at[n], gather_got.at[n]).wait_send()

    def far_first(do):
        def step(k, carry):
            do(k)
            return carry

        lax.fori_loop(1, cells, step, 0)

    def mine(n):
        return lax.rem(cell - groups * n + 4 * cells, cells)

    def scatter_start(n):
        pair(n).wait()
        summed[n] = part[n, core] + mates[n]

        def send(k):
            to = lax.rem(cell + k, cells)
            j = lax.rem(to - groups * n + 4 * cells, cells)

            @pl.when(j < groups)
            def _():
                scatter(n, to, j).start()

        far_first(send)

    def gather_start(n):
        j = mine(n)

        @pl.when(j < groups)
        def _():
            total = summed[n, j]
            whole(terms.at[n, pl.ds(1, cells - 1)], scatter_sent.at[n], scatter_got.at[n]).wait_recv()
            for k in range(1, cells):
                total = total + terms[n, k]
            own[n] = total * scale
            far_first(lambda k: gather(n, k, j).start())
            full[n, core, j] = own[n]

    def pair_back_start(n):
        gather_got_wait(n)
        pair_back(n).start()

    def finish(n, p):
        pair_back(n).wait()
        give(n, p)

    fetches[3].wait()
    lax.fori_loop(0, LEAVES, inner, 0)
    lax.fori_loop(0, SIDE // 2, turn, 0)
    gradient(0, 0, 0, 4)
    lay(0)
    pair(0).start()
    gradient(1, -1, 1, 3)
    gradient(2, 1, 0, 3)
    scatter_start(0)
    copy_up.wait()
    copy_down.wait()
    for s in range(LEAVES):
        high[LEAVES + s] = got_high[s].astype(F32).reshape(SIDE, SIDE, 128)
        low[LEAVES + s] = got_low[s].astype(F32).reshape(SIDE, SIDE, 128)

    def outer(s, carry):
        for p, row, pool in ((-1, 0, high), (1, SIDE + 1, low)):
            ids = {(q + 1, r + 1): source(s, p, q, r) for q in (-1, 0, 1) for r in (-1, 0, 1)}
            build(s, row, lambda i, lo, hi, pool=pool: pool[i, lo:hi], ids)
        return carry

    lax.fori_loop(0, LEAVES, outer, 0)

    half = lax.broadcasted_iota(jnp.int32, (WIDE, 128), 1) < CH

    def convolve(s, carry):
        xs, ds = [], []
        for n in range(3):
            one = a0[n : n + SIDE, s].reshape(WIDE, 128)
            two = a1[n : n + SIDE, s].reshape(WIDE, 128)
            three = a2[n : n + SIDE, s].reshape(WIDE, 128)
            xs += [one, three]
            ds += [two, three]
        yo = jnp.dot(jnp.concatenate(xs, axis=1), wf[...], preferred_element_type=F32)
        yb = jnp.dot(jnp.concatenate(ds, axis=1), wb[...], preferred_element_type=F32)
        shape = (SIDE, 10, SIDE, 128)
        ahead = (yo[:, 128:] + yb[:, 128:]).reshape(shape)
        behind = jnp.where(half, yo[:, :128], yb[:, :128]).reshape(shape)
        level = pltpu.roll(jnp.where(half, yb[:, :128], yo[:, :128]), CH, 1).reshape(shape)
        total = behind[:, 0:8] + level[:, 1:9] + ahead[:, 2:10]
        turned = total.reshape(VOX, 128).T * occ[s]
        out_ref[s] = turned[:CH].astype(BF16)
        back_ref[s] = turned[CH:].astype(BF16)
        return carry

    sums[1] += planes(-1, 0, 1)
    lay(1)
    pair(1).start()
    sums[2] += planes(1, SIDE - 1, 1)
    lay(2)
    pair(2).start()

    fetches[4].wait()

    def weight(p, q, r):
        return w_ref[tap(p, q, r)].astype(F32)

    for n, p in enumerate((-1, 0, 1)):
        rows = []
        for r in (-1, 0, 1):
            rows.append(
                jnp.concatenate([weight(p, -1, r), weight(p, 0, r), weight(p, 1, r), none], axis=1)
            )
        rows.append(jnp.zeros((CH, 4 * CH), F32))
        wf[n * 256 : (n + 1) * 256] = jnp.concatenate(rows, axis=0).astype(BF16)
        cols = []
        for q in (0, -1, None, 1):
            if q is None:
                cols.append(jnp.zeros((CH, 4 * CH), F32))
            else:
                cols.append(
                    jnp.concatenate(
                        [weight(-p, -q, 0), weight(-p, -q, 1), none, weight(-p, -q, -1)], axis=1
                    )
                )
        wb[n * 256 : (n + 1) * 256] = jnp.concatenate(cols, axis=0).T.astype(BF16)

    scatter_start(1)
    scatter_start(2)
    gather_start(0)
    lax.fori_loop(0, 6, convolve, 0)
    gather_start(1)
    gather_start(2)
    lax.fori_loop(6, 8, convolve, 0)
    leave = [
        pltpu.make_async_copy(out_ref, out_hbm, out_sems.at[0]),
        pltpu.make_async_copy(back_ref, back_hbm, out_sems.at[1]),
    ]
    leave[0].start()
    leave[1].start()

    def grad_leave(n, p):
        rows = pl.ds(9 * (p + 1), 9)
        leave.append(
            pltpu.make_async_copy(grad_ref.at[rows], grad_hbm.at[rows], out_sems.at[2 + n])
        )
        leave[-1].start()

    for n in range(3):
        scatter_sent_wait(n)
    pair_back_start(0)
    finish(0, 0)
    grad_leave(0, 0)
    pair_back_start(1)
    pair_back_start(2)
    for n in range(3):
        gather_sent_wait(n)
    finish(1, -1)
    grad_leave(1, -1)
    finish(2, 1)
    grad_leave(2, 1)
    for copy in leave:
        copy.wait()


PIECES = ((0, 0, 4), (0, 4, 4), (1, 0, 4), (1, 4, 4), (2, 0, 9), (2, 9, 9), (2, 18, 9))


def write_out(*refs):
    sems = refs[9]
    ins, outs = [], []
    for n, (which, start, count) in enumerate(PIECES):
        rows = pl.ds(start, count)
        source, dest, held = (refs[which + m].at[rows] for m in (0, 3, 6))
        ins.append(pltpu.make_async_copy(source, held, sems.at[0, n]))
        outs.append(pltpu.make_async_copy(held, dest, sems.at[1, n]))
    for copy in ins:
        copy.start()
    for n, copy in enumerate(ins):
        copy.wait()
        outs[n].start()
    for copy in outs:
        copy.wait()


def shards(cells, features, cotangent, weight, mask_words, neighbors):
    scale = float(cells * 2 * LEAVES * VOX) ** -0.5
    vmem = pltpu.VMEM
    dma = pltpu.SemaphoreType.DMA
    in_hbm = pl.BlockSpec(memory_space=pltpu.HBM)
    field = jax.ShapeDtypeStruct((LEAVES, CH, VOX), BF16)
    results = (field, field, jax.ShapeDtypeStruct((27, CH, CH), F32))
    per = -(-18 // cells)
    groups = 18 // per
    tiles = (groups, per, 8, 128)
    made = pl.pallas_call(
        functools.partial(kernel, cells, scale),
        out_shape=results,
        in_specs=[in_hbm] * 5,
        out_specs=(in_hbm,) * 3,
        scratch_shapes=[
            vmem((LEAVES, CH, VOX), BF16),
            vmem((LEAVES, CH, VOX), BF16),
            vmem((27, CH, CH), F32),
            vmem((LEAVES, CH, VOX), BF16),
            vmem((LEAVES, CH, VOX), BF16),
            vmem((27, CH, CH), BF16),
            vmem(mask_words.shape, jnp.int32),
            pltpu.SMEM(neighbors.shape, jnp.int32),
            vmem((LEAVES, 1, VOX), F32),
            vmem((LEAVES + 1, SIDE, SIDE, SIDE, 128), F32),
            vmem((2 * LEAVES + 1, SIDE, SIDE, 128), F32),
            vmem((2 * LEAVES + 1, SIDE, SIDE, 128), F32),
            vmem((LEAVES, PLANE, 128), BF16),
            vmem((LEAVES, PLANE, 128), BF16),
            vmem((LEAVES, PLANE, 128), BF16),
            vmem((LEAVES, PLANE, 128), BF16),
            vmem((10, LEAVES, ROWS, 128), BF16),
            vmem((10, LEAVES, ROWS, 128), BF16),
            vmem((10, LEAVES, ROWS, 128), BF16),
            vmem((3 * CH, LEAVES * WIDE), BF16),
            vmem((768, 256), BF16),
            vmem((768, 256), BF16),
            vmem((256, 192), F32),
            vmem((3, 192, 256), F32),
            vmem((3, 2) + tiles, F32),
            vmem((3,) + tiles, F32),
            vmem((3,) + tiles, F32),
            vmem((3, cells) + tiles[1:], F32),
            vmem((3,) + tiles[1:], F32),
            vmem((3, 2) + tiles, F32),
            dma((5,)),
            dma((5,)),
            dma((2, 2)),
            dma((4, 3)),
            dma((3,)),
            dma((3,)),
            dma((3,)),
            dma((3,)),
        ],
        compiler_params=pltpu.CompilerParams(
            collective_id=0, has_side_effects=True, vmem_limit_bytes=60_000_000
        ),
        name="sparse_conv",
    )(features, cotangent, weight, mask_words, neighbors)
    return pl.pallas_call(
        write_out,
        out_shape=results,
        in_specs=[in_hbm] * 3,
        out_specs=(in_hbm,) * 3,
        scratch_shapes=[vmem(r.shape, r.dtype) for r in results] + [dma((2, len(PIECES)))],
        compiler_params=pltpu.CompilerParams(vmem_limit_bytes=60_000_000),
        name="write_out",
    )(*made)


def solution(mesh):
    placed = (
        P(("scene", "dom"), None, None),
        P(("scene", "dom"), None, None),
        P(),
        P(("scene", "dom"), None),
        P(("scene", "dom"), None),
    )
    return jax.shard_map(
        functools.partial(shards, mesh.shape["dom"] // 2),
        mesh=mesh,
        in_specs=placed,
        out_specs=(
            P(("scene", "dom"), None, None),
            P(("scene", "dom"), None, None),
            P("scene", None, None),
        ),
        check_vma=False,
    )
```

time: 50.1 us -> 41.5 us (0.83)
  local copies, waits for them, and re-layouts: 6.96 us -> 0 us
  Pallas kernels: 42.3 us -> 40.8 us
    unnamed x13 -> x0, local copies, waits for them, and re-layouts: 6.96 us -> none
    pallas_call x1 -> x2, Pallas kernels: 42.3 us -> 40.8 us  [the longest x1 38.4 us: shards(): pl.pallas_call(functools.partial(kernel, cells, scale), out_shape=results...]
where the time goes in v2:
time: 41.5 us; the launch traced here: 41.4 us
  Pallas kernels  40.8 us (98%)
  between operations  0.64 us (2%)
    pallas_call x1, Pallas kernels, shards(): pl.pallas_call(functools.partial(kernel, cells, scale), out_shape=results...  38.4 us
    pallas_call x1, Pallas kernels, shards(): pl.pallas_call(write_out, out_shape=results, in_specs=[in_hbm] * 3, out_s...  2.33 us

profile of v2, /device:TPU:1, one launch (start us, length us, event | category | flops | bytes accessed | tf_op | source)
XLA Modules:
  0.0 41.4 jit_solution(8078957051626917852)
XLA Ops:
  0.6 38.4 %sparse_conv.1 = (bf16[8,64,512]{2,1,0:T(8,128)(2,1)}, bf16[8,64,512]{2,1,0:T(8,128)(2,1)}, f32[27,64,64]{2,1,0:T(8,128)}) custom-call(bf16[8,64,512]{2,1,0:T(8,128)(2,1)} %x_hbm.1, bf16[8,64,512]{2,1,0:T(8,128)(2,1)} %dy_hbm.1, bf16[27,64,64]{2,1,0:T(8,128)(2,1)} %w_hbm.1, s32[8,18]{1,0:T(8,128)} %words_hbm.1, s32[8,26]{1,0:T(8,128)} %near_hbm.1), custom_call_target="tpu_custom_call" | custom-call | tf_op jit(solution)/shard_map/sparse_conv/pallas_call | solution.py:512
  39.1 2.3 %write_out.1 = (bf16[8,64,512]{2,1,0:T(8,128)(2,1)}, bf16[8,64,512]{2,1,0:T(8,128)(2,1)}, f32[27,64,64]{2,1,0:T(8,128)}) custom-call(bf16[8,64,512]{2,1,0:T(8,128)(2,1)} %get-tuple-element.6.refs_0_, bf16[8,64,512]{2,1,0:T(8,128)(2,1)} %get-tuple-element.7.refs_1_, f32[27,64,64]{2,1,0:T(8,128)} %get-tuple-element.8.refs_2_), custom_call_target="tpu_custom_call" | custom-call | tf_op jit(solution)/shard_map/write_out/pallas_call | solution.py:562

commit v3 on v2

--- a/solution.py
+++ b/solution.py
@@ -148,11 +148,6 @@
     high[2 * LEAVES] = jnp.zeros((SIDE, SIDE, 128), F32)
     low[2 * LEAVES] = jnp.zeros((SIDE, SIDE, 128), F32)
 
-    pl.semaphore_wait(barrier, cells + 2)
-    copy_up = copy_to(send_high, got_high, halo_sems.at[0, 0], halo_sems.at[0, 1], up)
-    copy_down = copy_to(send_low, got_low, halo_sems.at[1, 0], halo_sems.at[1, 1], down)
-    copy_up.start()
-    copy_down.start()
 
     none = jnp.zeros((CH, CH), F32)
     sub = lax.broadcasted_iota(jnp.int32, (10, SIDE, 128), 1)
@@ -365,8 +360,19 @@
         give(n, p)
 
     fetches[3].wait()
-    lax.fori_loop(0, LEAVES, inner, 0)
-    lax.fori_loop(0, SIDE // 2, turn, 0)
+    def local(h, carry):
+        turn(h, carry)
+        inner(2 * h, carry)
+        inner(2 * h + 1, carry)
+        return carry
+
+    lax.fori_loop(0, LEAVES // 2, local, 0)
+
+    pl.semaphore_wait(barrier, cells + 2)
+    copy_up = copy_to(send_high, got_high, halo_sems.at[0, 0], halo_sems.at[0, 1], up)
+    copy_down = copy_to(send_low, got_low, halo_sems.at[1, 0], halo_sems.at[1, 1], down)
+    copy_up.start()
+    copy_down.start()
     gradient(0, 0, 0, 4)
     lay(0)
     pair(0).start()

time: 41.5 us -> 38.7 us (0.933)
  Pallas kernels: 40.8 us -> 37.9 us
    pallas_call x1, Pallas kernels: 38.4 us -> 35.6 us  [shards(): pl.pallas_call(functools.partial(kernel, cells, scale), out_shape=results...]
where the time goes in v3:
time: 38.7 us; the launch traced here: 38.6 us
  Pallas kernels  37.9 us (98%)
  between operations  0.64 us (2%)
    pallas_call x1, Pallas kernels, shards(): pl.pallas_call(functools.partial(kernel, cells, scale), out_shape=results...  35.6 us
    pallas_call x1, Pallas kernels, shards(): pl.pallas_call(write_out, out_shape=results, in_specs=[in_hbm] * 3, out_s...  2.33 us

profile of v3, /device:TPU:1, one launch (start us, length us, event | category | flops | bytes accessed | tf_op | source)
XLA Modules:
  0.0 38.6 jit_solution(10253798930787807763)
XLA Ops:
  0.6 35.6 %sparse_conv.1 = (bf16[8,64,512]{2,1,0:T(8,128)(2,1)}, bf16[8,64,512]{2,1,0:T(8,128)(2,1)}, f32[27,64,64]{2,1,0:T(8,128)}) custom-call(bf16[8,64,512]{2,1,0:T(8,128)(2,1)} %x_hbm.1, bf16[8,64,512]{2,1,0:T(8,128)(2,1)} %dy_hbm.1, bf16[27,64,64]{2,1,0:T(8,128)(2,1)} %w_hbm.1, s32[8,18]{1,0:T(8,128)} %words_hbm.1, s32[8,26]{1,0:T(8,128)} %near_hbm.1), custom_call_target="tpu_custom_call" | custom-call | tf_op jit(solution)/shard_map/sparse_conv/pallas_call | solution.py:518
  36.2 2.3 %write_out.1 = (bf16[8,64,512]{2,1,0:T(8,128)(2,1)}, bf16[8,64,512]{2,1,0:T(8,128)(2,1)}, f32[27,64,64]{2,1,0:T(8,128)}) custom-call(bf16[8,64,512]{2,1,0:T(8,128)(2,1)} %get-tuple-element.6.refs_0_, bf16[8,64,512]{2,1,0:T(8,128)(2,1)} %get-tuple-element.7.refs_1_, f32[27,64,64]{2,1,0:T(8,128)} %get-tuple-element.8.refs_2_), custom_call_target="tpu_custom_call" | custom-call | tf_op jit(solution)/shard_map/write_out/pallas_call | solution.py:568

commit v4 on v3

--- a/solution.py
+++ b/solution.py
@@ -422,6 +422,8 @@
     lay(2)
     pair(2).start()
 
+    scatter_start(1)
+    scatter_start(2)
     fetches[4].wait()
 
     def weight(p, q, r):
@@ -447,8 +449,6 @@
                 )
         wb[n * 256 : (n + 1) * 256] = jnp.concatenate(cols, axis=0).T.astype(BF16)
 
-    scatter_start(1)
-    scatter_start(2)
     gather_start(0)
     lax.fori_loop(0, 6, convolve, 0)
     gather_start(1)
@@ -485,23 +485,12 @@
         copy.wait()
 
 
-PIECES = ((0, 0, 4), (0, 4, 4), (1, 0, 4), (1, 4, 4), (2, 0, 9), (2, 9, 9), (2, 18, 9))
-
-
 def write_out(*refs):
-    sems = refs[9]
-    ins, outs = [], []
-    for n, (which, start, count) in enumerate(PIECES):
-        rows = pl.ds(start, count)
-        source, dest, held = (refs[which + m].at[rows] for m in (0, 3, 6))
-        ins.append(pltpu.make_async_copy(source, held, sems.at[0, n]))
-        outs.append(pltpu.make_async_copy(held, dest, sems.at[1, n]))
-    for copy in ins:
+    sems = refs[6]
+    copies = [pltpu.make_async_copy(refs[n], refs[n + 3], sems.at[n]) for n in range(3)]
+    for copy in copies:
         copy.start()
-    for n, copy in enumerate(ins):
-        copy.wait()
-        outs[n].start()
-    for copy in outs:
+    for copy in copies:
         copy.wait()
 
 
@@ -510,6 +499,7 @@
     vmem = pltpu.VMEM
     dma = pltpu.SemaphoreType.DMA
     in_hbm = pl.BlockSpec(memory_space=pltpu.HBM)
+    anywhere = pl.BlockSpec(memory_space=pl.ANY)
     field = jax.ShapeDtypeStruct((LEAVES, CH, VOX), BF16)
     results = (field, field, jax.ShapeDtypeStruct((27, CH, CH), F32))
     per = -(-18 // cells)
@@ -519,7 +509,7 @@
         functools.partial(kernel, cells, scale),
         out_shape=results,
         in_specs=[in_hbm] * 5,
-        out_specs=(in_hbm,) * 3,
+        out_specs=(anywhere,) * 3,
         scratch_shapes=[
             vmem((LEAVES, CH, VOX), BF16),
             vmem((LEAVES, CH, VOX), BF16),
@@ -561,17 +551,17 @@
             dma((3,)),
         ],
         compiler_params=pltpu.CompilerParams(
-            collective_id=0, has_side_effects=True, vmem_limit_bytes=60_000_000
+            collective_id=0, has_side_effects=True, vmem_limit_bytes=54_000_000
         ),
         name="sparse_conv",
-    )(features, cotangent, weight, mask_words, neighbors)
+    )(*(pltpu.with_memory_space_constraint(a, pltpu.HBM) for a in (features, cotangent, weight, mask_words, neighbors)))
     return pl.pallas_call(
         write_out,
         out_shape=results,
-        in_specs=[in_hbm] * 3,
+        in_specs=[anywhere] * 3,
         out_specs=(in_hbm,) * 3,
-        scratch_shapes=[vmem(r.shape, r.dtype) for r in results] + [dma((2, len(PIECES)))],
-        compiler_params=pltpu.CompilerParams(vmem_limit_bytes=60_000_000),
+        scratch_shapes=[dma((3,))],
+        compiler_params=pltpu.CompilerParams(vmem_limit_bytes=1_000_000),
         name="write_out",
     )(*made)
 

time: 38.7 us -> 37 us (0.956)
  Pallas kernels: 37.9 us -> 36.2 us
    pallas_call x1, Pallas kernels: 2.33 us -> 1.29 us  [shards(): pl.pallas_call(write_out, out_shape=results, in_specs=[anywhere] * 3, out...]
    pallas_call x1, Pallas kernels: 35.6 us -> 35 us  [shards(): pl.pallas_call(functools.partial(kernel, cells, scale), out_shape=results...]
where the time goes in v4:
time: 37 us; the launch traced here: 36.9 us
  Pallas kernels  36.2 us (98%)
  between operations  0.64 us (2%)
    pallas_call x1, Pallas kernels, shards(): pl.pallas_call(functools.partial(kernel, cells, scale), out_shape=results...  35 us
    pallas_call x1, Pallas kernels, shards(): pl.pallas_call(write_out, out_shape=results, in_specs=[anywhere] * 3, out...  1.29 us

profile of v4, /device:TPU:1, one launch (start us, length us, event | category | flops | bytes accessed | tf_op | source)
XLA Modules:
  0.0 36.9 jit_solution(9614137172427251630)
XLA Ops:
  0.6 35.0 %sparse_conv.1 = (bf16[8,64,512]{2,1,0:T(8,128)(2,1)S(1)}, bf16[8,64,512]{2,1,0:T(8,128)(2,1)S(1)}, f32[27,64,64]{2,1,0:T(8,128)S(1)}) custom-call(bf16[8,64,512]{2,1,0:T(8,128)(2,1)} %x_hbm.1, bf16[8,64,512]{2,1,0:T(8,128)(2,1)} %dy_hbm.1, bf16[27,64,64]{2,1,0:T(8,128)(2,1)} %w_hbm.1, s32[8,18]{1,0:T(8,128)} %words_hbm.1, s32[8,26]{1,0:T(8,128)} %near_hbm.1), custom_call_target="tpu_custom_call" | custom-call | tf_op jit(solution)/shard_map/sparse_conv/pallas_call | solution.py:508
  35.6 1.3 %write_out.1 = (bf16[8,64,512]{2,1,0:T(8,128)(2,1)}, bf16[8,64,512]{2,1,0:T(8,128)(2,1)}, f32[27,64,64]{2,1,0:T(8,128)}) custom-call(bf16[8,64,512]{2,1,0:T(8,128)(2,1)S(1)} %get-tuple-element.6.refs_0_, bf16[8,64,512]{2,1,0:T(8,128)(2,1)S(1)} %get-tuple-element.7.refs_1_, f32[27,64,64]{2,1,0:T(8,128)S(1)} %get-tuple-element.8.refs_2_), custom_call_target="tpu_custom_call" | custom-call | tf_op jit(solution)/shard_map/write_out/pallas_call | solution.py:558

commit v5 on v4

--- a/solution.py
+++ b/solution.py
@@ -42,9 +42,6 @@
     w_hbm,
     words_hbm,
     near_hbm,
-    out_hbm,
-    back_hbm,
-    grad_hbm,
     out_ref,
     back_ref,
     grad_ref,
@@ -76,7 +73,6 @@
     own,
     full,
     in_sems,
-    out_sems,
     halo_sems,
     core_sems,
     scatter_sent,
@@ -454,35 +450,16 @@
     gather_start(1)
     gather_start(2)
     lax.fori_loop(6, 8, convolve, 0)
-    leave = [
-        pltpu.make_async_copy(out_ref, out_hbm, out_sems.at[0]),
-        pltpu.make_async_copy(back_ref, back_hbm, out_sems.at[1]),
-    ]
-    leave[0].start()
-    leave[1].start()
-
-    def grad_leave(n, p):
-        rows = pl.ds(9 * (p + 1), 9)
-        leave.append(
-            pltpu.make_async_copy(grad_ref.at[rows], grad_hbm.at[rows], out_sems.at[2 + n])
-        )
-        leave[-1].start()
-
     for n in range(3):
         scatter_sent_wait(n)
     pair_back_start(0)
     finish(0, 0)
-    grad_leave(0, 0)
     pair_back_start(1)
     pair_back_start(2)
     for n in range(3):
         gather_sent_wait(n)
     finish(1, -1)
-    grad_leave(1, -1)
     finish(2, 1)
-    grad_leave(2, 1)
-    for copy in leave:
-        copy.wait()
 
 
 def write_out(*refs):
@@ -509,11 +486,8 @@
         functools.partial(kernel, cells, scale),
         out_shape=results,
         in_specs=[in_hbm] * 5,
-        out_specs=(anywhere,) * 3,
+        out_specs=(pl.BlockSpec(memory_space=pltpu.VMEM),) * 3,
         scratch_shapes=[
-            vmem((LEAVES, CH, VOX), BF16),
-            vmem((LEAVES, CH, VOX), BF16),
-            vmem((27, CH, CH), F32),
             vmem((LEAVES, CH, VOX), BF16),
             vmem((LEAVES, CH, VOX), BF16),
             vmem((27, CH, CH), BF16),
@@ -542,7 +516,6 @@
             vmem((3,) + tiles[1:], F32),
             vmem((3, 2) + tiles, F32),
             dma((5,)),
-            dma((5,)),
             dma((2, 2)),
             dma((4, 3)),
             dma((3,)),

time: 37 us -> 36.9 us (level)
  no operation moved by 1% of the time
where the time goes in v5:
time: 36.9 us; the launch traced here: 36.8 us
  Pallas kernels  36.1 us (98%)
  between operations  0.64 us (2%)
    pallas_call x1, Pallas kernels, shards(): pl.pallas_call(functools.partial(kernel, cells, scale), out_shape=results...  34.8 us
    pallas_call x1, Pallas kernels, shards(): pl.pallas_call(write_out, out_shape=results, in_specs=[anywhere] * 3, out...  1.29 us

profile of v5, /device:TPU:1, one launch (start us, length us, event | category | flops | bytes accessed | tf_op | source)
XLA Modules:
  0.0 36.8 jit_solution(14220868889070331383)
XLA Ops:
  0.6 34.8 %sparse_conv.1 = (bf16[8,64,512]{2,1,0:T(8,128)(2,1)S(1)}, bf16[8,64,512]{2,1,0:T(8,128)(2,1)S(1)}, f32[27,64,64]{2,1,0:T(8,128)S(1)}) custom-call(bf16[8,64,512]{2,1,0:T(8,128)(2,1)} %x_hbm.1, bf16[8,64,512]{2,1,0:T(8,128)(2,1)} %dy_hbm.1, bf16[27,64,64]{2,1,0:T(8,128)(2,1)} %w_hbm.1, s32[8,18]{1,0:T(8,128)} %words_hbm.1, s32[8,26]{1,0:T(8,128)} %near_hbm.1), custom_call_target="tpu_custom_call" | custom-call | tf_op jit(solution)/shard_map/sparse_conv/pallas_call | solution.py:485
  35.5 1.3 %write_out.1 = (bf16[8,64,512]{2,1,0:T(8,128)(2,1)}, bf16[8,64,512]{2,1,0:T(8,128)(2,1)}, f32[27,64,64]{2,1,0:T(8,128)}) custom-call(bf16[8,64,512]{2,1,0:T(8,128)(2,1)S(1)} %get-tuple-element.6.refs_0_, bf16[8,64,512]{2,1,0:T(8,128)(2,1)S(1)} %get-tuple-element.7.refs_1_, f32[27,64,64]{2,1,0:T(8,128)S(1)} %get-tuple-element.8.refs_2_), custom_call_target="tpu_custom_call" | custom-call | tf_op jit(solution)/shard_map/write_out/pallas_call | solution.py:531
